TPU v7x, 32 devices: a whole 2x2x4 slice. The times are simulated.
32 devices in a mesh: rows: 16 (over z, y, core), rep: 2 (over x).
Axes of the slice: x: 2, y: 2, z: 4, core: 2. Of those that a mesh axis runs over, the one named last changes fastest.
Arguments:
- embeddings: bfloat16 [11264, 1024], P(('rows', 'rep')), may hold values from -6 to 6
- owner_ids: int32 [11264, 1], P(('rows', 'rep')), may hold values from 0 to 15; in each aligned block of 352 rows (0 to 351, 352 to 703, ...) at most 64 rows name the same one
- live_mask: int32 [11264], P(('rows', 'rep')), may hold values 0 or 1
Outputs:
- neighbour_means: bfloat16 [11264, 1024], P(('rows', 'rep'))
Inputs may be any that keep to these rules, and one draw needn't show every extreme that they name: `owner_ids`: among the rows of one device, at most 64 name the same owner, and in every draw some owner is named by exactly 64 of them.
All inputs are finite; a program needn't handle non-finite values. Where the computation divides by a largest or mean magnitude, that divisor is 1e-20 or more. No bound on the sum of `live_mask` on one device may be relied on, other than what follows from the above.
Results may differ from a plain program's by a relative error of at most 0.0017.
The roundings to bfloat16 on the way count: a program that leaves them out, or rounds other values in their place, can miss the bound.
Values may be sent and summed in bfloat16 or wider, within the bound.
A program may use at most 64 MiB of HBM per device.

v0:
```python
import jax
import jax.numpy as jnp
from jax import lax
from jax.sharding import PartitionSpec as P

BUCKET = 1024
KERNEL_SCALE = 4.0
EPSILON = 1e-06
PRECISE = lax.Precision.HIGHEST


def block_positions(owner_block, owners, slot_cap):
    onehot = (owner_block[:, None] == jnp.arange(owners, dtype=jnp.int32)[None, :]).astype(
        jnp.int32
    )
    before = jnp.cumsum(onehot, axis=0) - onehot
    slot_rank = jnp.sum(before * onehot, axis=1)
    return owner_block * slot_cap + slot_rank


def whiten(embedded, inverse_root):
    mapped = jnp.dot(embedded, inverse_root, preferred_element_type=jnp.float32)
    return (mapped * lax.rsqrt(jnp.mean(mapped * mapped, axis=1, keepdims=True) + EPSILON)).astype(
        jnp.bfloat16
    )


def bucket_means(members, alive):
    scores = jnp.dot(members, members.T, preferred_element_type=jnp.float32)
    weights = jnp.exp(KERNEL_SCALE * (scores / members.shape[1] - 1.0)) * alive[None, :]
    denominator = jnp.sum(weights, axis=1, keepdims=True)
    summed = jnp.dot(weights.astype(jnp.bfloat16), members, preferred_element_type=jnp.float32)
    averaged = summed / jnp.where(alive[:, None] > 0, denominator, 1.0)
    normed = averaged * lax.rsqrt(jnp.mean(averaged * averaged, axis=1, keepdims=True) + EPSILON)
    return (normed * alive[:, None]).astype(jnp.bfloat16)


def spread(values, positions, slots_all):
    return jnp.zeros((slots_all,) + values.shape[1:], values.dtype).at[positions].set(values)


def first_rows(start_y, first_row, row_share):
    y_rows = lax.dynamic_slice_in_dim(start_y, first_row, row_share, 0)
    return 0.5 * (3.0 * y_rows - jnp.dot(y_rows, start_y, precision=PRECISE))


def second_rows(next_y, next_z, first_row, row_share):
    z_rows = lax.dynamic_slice_in_dim(next_z, first_row, row_share, 0)
    product = jnp.dot(z_rows, next_y, precision=PRECISE)
    return 0.5 * (3.0 * z_rows - jnp.dot(product, next_z, precision=PRECISE))


def per_device(embeddings, owner_ids, live_mask):
    rows_here, columns = embeddings.shape
    owners = lax.axis_size("rows")
    slot_cap = BUCKET // owners
    positions = block_positions(owner_ids[:, 0], owners, slot_cap)
    live_rows = live_mask.astype(jnp.bfloat16)
    masked = embeddings * live_rows[:, None]
    partial_moment = lax.dot_general(
        masked, masked, (((0,), (0,)), ((), ())), preferred_element_type=jnp.float32
    )
    moment = lax.psum(partial_moment, ("rows", "rep"))
    start_y = moment / jnp.max(jnp.sum(jnp.abs(moment), axis=1))
    next_z = 0.5 * (3.0 * jnp.eye(columns, dtype=jnp.float32) - start_y)
    row_share = columns // lax.axis_size("rep")
    first_row = lax.axis_index("rep") * row_share
    next_y = lax.all_gather(first_rows(start_y, first_row, row_share), "rep", axis=0, tiled=True)
    inverse_root = lax.all_gather(
        second_rows(next_y, next_z, first_row, row_share).astype(jnp.bfloat16),
        "rep",
        axis=0,
        tiled=True,
    )
    whitened = whiten(embeddings, inverse_root)
    sent_rows, sent_live = (
        lax.all_to_all(
            spread(whitened, positions, BUCKET).reshape(owners, slot_cap, columns),
            "rows",
            split_axis=0,
            concat_axis=0,
            tiled=True,
        ),
        lax.all_to_all(
            spread(live_rows, positions, BUCKET).reshape(owners, slot_cap),
            "rows",
            split_axis=0,
            concat_axis=0,
            tiled=True,
        ),
    )
    members = sent_rows.reshape(BUCKET, columns)
    member_live = sent_live.reshape(BUCKET).astype(jnp.float32)
    means = bucket_means(members, member_live)
    returned = lax.all_to_all(
        means.reshape(owners, slot_cap, columns), "rows", split_axis=0, concat_axis=0, tiled=True
    )
    return returned.reshape(BUCKET, columns)[positions]


def solution(mesh):
    placed = (P(("rows", "rep"), None), P(("rows", "rep"), None), P(("rows", "rep")))
    return jax.shard_map(
        per_device, mesh=mesh, in_specs=placed, out_specs=P(("rows", "rep"), None), check_vma=False
    )
```

profile of v0, /device:TPU:13, one launch (start us, length us, event | category | flops | bytes accessed | tf_op | source)
XLA Modules:
  0.0 409.3 jit_solution(2860625432853445525)
XLA Ops:
  6.5 0.7 convert_element_type.41
  7.2 4.6 %fusion.21 = f32[1024,1024]{1,0:T(8,128)} fusion(bf16[352,1024]{1,0:T(8,128)(2,1)} %param.3, bf16[352]{0:T(512)(128)(2,1)S(1)} %convert_element_type.41), kind=kOutput, calls=%fused_computation.30 | convolution fusion | flops 738557952 | bytes 4915904 | tf_op jit(solution)/shard_map/dot_general | solution.py:60
  11.9 141.8 %all-reduce.3.cloned.1.call-done = f32[1024,1024]{1,0:T(8,128)} async-done(((f32[1024,1024]{1,0:T(8,128)}), f32[1024,1024]{1,0:T(8,128)}) %all-reduce.3.cloned.1.call-update) | async-done | bytes 4194320 | tf_op jit(solution)/shard_map/psum | solution.py:63
  153.8 2.6 abs_reduce_fusion
  156.9 5.7 %subtract_multiply_fusion = (f32[1024,1024]{1,0:T(8,128)}, f32[1024,1024]{1,0:T(8,128)S(1)}) fusion(f32[1024,1024]{1,0:T(8,128)} %all-reduce.3.cloned.1.call-done, f32[]{:T(128)} %reduce_max.9), kind=kLoop, calls=%fused_computation.6 | loop fusion | flops 5242880 | bytes 12582916 | tf_op jit(solution)/shard_map/mul | solution.py:65
  162.7 8.4 %subtract_multiply_fusion.1 = f32[512,1024]{1,0:T(8,128)} fusion(f32[1024,1024]{1,0:T(8,128)S(1)} %get-tuple-element.6, s32[]{:T(128)S(6)} %select_n.20), kind=kOutput, calls=%fused_computation.18 | convolution fusion | flops 6444023808 | bytes 10486784 | tf_op jit(solution)/shard_map/dot_general | solution.py:44
  171.3 57.7 %all-gather.3.cloned.1.call-done = f32[1024,1024]{1,0:T(8,128)} async-done(((f32[512,1024]{1,0:T(8,128)}), f32[1024,1024]{1,0:T(8,128)}) %all-gather.3.cloned.1.call-update) | async-done | bytes 4194320 | tf_op jit(solution)/shard_map/all_gather | solution.py:68
  229.0 10.0 %fusion.10 = f32[512,1024]{1,0:T(8,128)S(1)} fusion(f32[1024,1024]{1,0:T(8,128)} %all-gather.3.cloned.1.call-done, f32[1024,1024]{1,0:T(8,128)} %get-tuple-element.5, s32[]{:T(128)S(6)} %select_n.20), kind=kOutput, calls=%fused_computation.22 | convolution fusion | flops 6442450944 | bytes 8388612 | tf_op jit(solution)/shard_map/dot_general | solution.py:49
  239.1 8.0 %multiply_convert_fusion.1 = bf16[512,1024]{1,0:T(8,128)(2,1)} fusion(f32[1024,1024]{1,0:T(8,128)S(1)} %copy-done, s32[]{:T(128)S(6)} %select_n.20, f32[512,1024]{1,0:T(8,128)S(1)} %fusion.10), kind=kOutput, calls=%fused_computation.17 | convolution fusion | flops 6444548096 | bytes 9437188 | tf_op jit(solution)/shard_map/dot_general | solution.py:50
  247.2 0.9 reduce-window.6
  248.5 2.8 scatter_custom_fusion.1
  251.2 0.7 all_to_all.16
  251.9 6.4 %all-to-all-start.1 = ((bf16[16,1,64]{2,1,0:T(2,128)(2,1)}), bf16[16,1,64]{2,1,0:T(2,128)(2,1)S(1)}, u32[]{:S(2)}, u32[]{:S(2)}) async-start(bf16[16,1,64]{2,1,0:T(2,128)(2,1)} %all_to_all.16), calls=%async_computation.1 | async-start | bytes 16384 | tf_op jit(solution)/shard_map/all_to_all | solution.py:84
  258.3 22.1 %all-gather.5.cloned.1.call-done = bf16[1024,1024]{1,0:T(8,128)(2,1)} async-done(((bf16[512,1024]{1,0:T(8,128)(2,1)}), bf16[1024,1024]{1,0:T(8,128)(2,1)}) %all-gather.5.cloned.1.call-update) | async-done | bytes 2097168 | tf_op jit(solution)/shard_map/all_gather | solution.py:69
  280.4 2.6 multiply_reduce_fusion.1
  283.0 3.7 scatter_custom_fusion
  286.7 6.4 %all-to-all-start = ((bf16[16,64,1024]{2,1,0:T(8,128)(2,1)}), bf16[16,64,1024]{2,1,0:T(8,128)(2,1)S(1)}, u32[]{:S(2)}, u32[]{:S(2)}) async-start(bf16[16,64,1024]{2,1,0:T(8,128)(2,1)} %bitcast.2), calls=%async_computation | async-start | bytes 4194304 | tf_op jit(solution)/shard_map/all_to_all | solution.py:77
  293.2 47.3 %all-to-all-done = bf16[16,64,1024]{2,1,0:T(8,128)(2,1)S(1)} async-done(((bf16[16,64,1024]{2,1,0:T(8,128)(2,1)}), bf16[16,64,1024]{2,1,0:T(8,128)(2,1)S(1)}, u32[]{:S(2)}, u32[]{:S(2)}) %all-to-all-start) | async-done | bytes 2097184 | tf_op jit(solution)/shard_map/all_to_all | solution.py:77
  340.5 2.7 fusion
  343.2 2.7 multiply_reduce_fusion
  346.0 1.8 multiply_convert_fusion
  347.8 4.9 %all-to-all-start.2 = ((bf16[16,64,1024]{2,1,0:T(8,128)(2,1)}), bf16[16,64,1024]{2,1,0:T(8,128)(2,1)S(1)}, u32[]{:S(2)}, u32[]{:S(2)}) async-start(bf16[16,64,1024]{2,1,0:T(8,128)(2,1)} %bitcast.30), calls=%async_computation.2 | async-start | bytes 4194304 | tf_op jit(solution)/shard_map/all_to_all | solution.py:95
  352.7 47.4 %all-to-all-done.2 = bf16[16,64,1024]{2,1,0:T(8,128)(2,1)S(1)} async-done(((bf16[16,64,1024]{2,1,0:T(8,128)(2,1)}), bf16[16,64,1024]{2,1,0:T(8,128)(2,1)S(1)}, u32[]{:S(2)}, u32[]{:S(2)}) %all-to-all-start.2) | async-done | bytes 2097184 | tf_op jit(solution)/shard_map/all_to_all | solution.py:95
  400.1 2.7 gather_fusion
  (28 shorter events, 1.5 us)
Async XLA Ops:
  6.5 147.2 %all-reduce.3.cloned.1.call-start = ((), (), s32[]{:S(2)}) async-start(), calls=%async_computation.3 | async-start | bytes 8388608 | tf_op jit(solution)/shard_map/psum | solution.py:63
  11.9 217.1 %all-gather.3.cloned.1.call-start = ((), (), s32[]{:S(2)}) async-start(), calls=%async_computation.4 | async-start | bytes 6291456 | tf_op jit(solution)/shard_map/all_gather | solution.py:68
  171.1 109.3 %all-gather.5.cloned.1.call-start = ((), (), s32[]{:S(2)}) async-start(), calls=%async_computation.5 | async-start | bytes 3145728 | tf_op jit(solution)/shard_map/all_gather | solution.py:69
  229.0 10.0 %copy-start = (f32[1024,1024]{1,0:T(8,128)S(1)}, f32[1024,1024]{1,0:T(8,128)}, u32[]{:S(2)}) copy-start(f32[1024,1024]{1,0:T(8,128)} %get-tuple-element.5) | copy-start | bytes 12582916
  239.0 8.1 %copy-start.2 = (s32[352,1]{0,1:T(1,128)S(1)}, s32[352,1]{0,1:T(1,128)}, u32[]{:S(2)}) copy-start(s32[352,1]{0,1:T(1,128)} %param.4) | copy-start | bytes 4228
  239.1 41.4 %copy-start.1 = (bf16[352,1024]{1,0:T(8,128)(2,1)S(1)}, bf16[352,1024]{1,0:T(8,128)(2,1)}, u32[]{:S(2)}) copy-start(bf16[352,1024]{1,0:T(8,128)(2,1)} %param.3) | copy-start | bytes 2162692
  251.9 34.8 %all-to-all-start.1 = ((bf16[16,1,64]{2,1,0:T(2,128)(2,1)}), bf16[16,1,64]{2,1,0:T(2,128)(2,1)S(1)}, u32[]{:S(2)}, u32[]{:S(2)}) async-start(bf16[16,1,64]{2,1,0:T(2,128)(2,1)} %all_to_all.16), calls=%async_computation.1 | async-start | bytes 16384 | tf_op jit(solution)/shard_map/all_to_all | solution.py:84
  286.7 53.8 %all-to-all-start = ((bf16[16,64,1024]{2,1,0:T(8,128)(2,1)}), bf16[16,64,1024]{2,1,0:T(8,128)(2,1)S(1)}, u32[]{:S(2)}, u32[]{:S(2)}) async-start(bf16[16,64,1024]{2,1,0:T(8,128)(2,1)} %bitcast.2), calls=%async_computation | async-start | bytes 4194304 | tf_op jit(solution)/shard_map/all_to_all | solution.py:77
  347.8 52.3 %all-to-all-start.2 = ((bf16[16,64,1024]{2,1,0:T(8,128)(2,1)}), bf16[16,64,1024]{2,1,0:T(8,128)(2,1)S(1)}, u32[]{:S(2)}, u32[]{:S(2)}) async-start(bf16[16,64,1024]{2,1,0:T(8,128)(2,1)} %bitcast.30), calls=%async_computation.2 | async-start | bytes 4194304 | tf_op jit(solution)/shard_map/all_to_all | solution.py:95
Sparse Core Ops, SparseCore 0:
  12.9 140.8 all-reduce.2
  171.2 57.7 all-gather.2
  247.3 33.1 all-gather.4
where the time goes:
time: 410 us; the launch traced here: 409 us
  waiting for transfers between devices  316 us (77%)
  matrix products  39.1 us (10%)
  starting transfers between devices  17.9 us (4%)
  other arithmetic  16.2 us (4%)
  between operations  13.2 us (3%)
  local copies, waits for them, and re-layouts  6.39 us (2%)
    psum x1, waiting for transfers between devices, per_device(): moment = lax.psum(partial_moment, ('rows', 'rep'))  142 us
    all_gather x1, waiting for transfers between devices, per_device(): lax.all_gather(first_rows(start_y, first_row, row_share), 'rep', axis=0,...  57.7 us
    all_to_all x1, waiting for transfers between devices, per_device(): lax.all_to_all(means.reshape(owners, slot_cap, columns), 'rows', split_ax...  47.4 us
    all_to_all x1, waiting for transfers between devices, per_device(): lax.all_to_all(spread(whitened, positions, BUCKET).reshape(owners, slot_c...  47.3 us
    all_gather x1, waiting for transfers between devices, per_device(): lax.all_gather(second_rows(next_y, next_z, first_row, row_share).astype(j...  22.1 us
    dot_general x1, matrix products, second_rows(): product = jnp.dot(z_rows, next_y, precision=PRECISE)  10 us
    dot_general x1, matrix products, first_rows(): return 0.5 * (3.0 * y_rows - jnp.dot(y_rows, start_y, precision=PRECISE))  8.4 us
  transfers between devices with their start and end apart: 6, of which 5 were waited for; matrix products, arithmetic and copies ran while one was open for 3% of the time, Pallas kernels for 0%

commit v1 on v0

--- a/solution.py
+++ b/solution.py
@@ -60,7 +60,7 @@
     partial_moment = lax.dot_general(
         masked, masked, (((0,), (0,)), ((), ())), preferred_element_type=jnp.float32
     )
-    moment = lax.psum(partial_moment, ("rows", "rep"))
+    moment = lax.psum(lax.psum(partial_moment, "rep"), "rows")
     start_y = moment / jnp.max(jnp.sum(jnp.abs(moment), axis=1))
     next_z = 0.5 * (3.0 * jnp.eye(columns, dtype=jnp.float32) - start_y)
     row_share = columns // lax.axis_size("rep")

time: 410 us -> 491 us (1.20)
  waiting for transfers between devices: 316 us -> 397 us
    psum x1 -> x2, waiting for transfers between devices: 142 us -> 223 us  [per_device(): moment = lax.psum(lax.psum(partial_moment, 'rep'), 'rows')]
  transfers between devices with their start and end apart: 6 -> 7, of which waited for: 5 -> 6; matrix products, arithmetic and copies ran while one was open for 3% -> 2% of each run, Pallas kernels for 0% -> 0%
where the time goes in v1:
time: 491 us; the launch traced here: 490 us
  waiting for transfers between devices  397 us (81%)
  matrix products  39.3 us (8%)
  starting transfers between devices  18 us (4%)
  other arithmetic  16.2 us (3%)
  between operations  13.2 us (3%)
  local copies, waits for them, and re-layouts  6.39 us (1%)
    psum x2, waiting for transfers between devices, per_device(): moment = lax.psum(lax.psum(partial_moment, 'rep'), 'rows')  223 us
    all_gather x1, waiting for transfers between devices, per_device(): lax.all_gather(first_rows(start_y, first_row, row_share), 'rep', axis=0,...  56.7 us
    all_to_all x1, waiting for transfers between devices, per_device(): lax.all_to_all(means.reshape(owners, slot_cap, columns), 'rows', split_ax...  47.4 us
    all_to_all x1, waiting for transfers between devices, per_device(): lax.all_to_all(spread(whitened, positions, BUCKET).reshape(owners, slot_c...  47.3 us
    all_gather x1, waiting for transfers between devices, per_device(): lax.all_gather(second_rows(next_y, next_z, first_row, row_share).astype(j...  22.1 us
    dot_general x1, matrix products, second_rows(): product = jnp.dot(z_rows, next_y, precision=PRECISE)  10 us
  transfers between devices with their start and end apart: 7, of which 6 were waited for; matrix products, arithmetic and copies ran while one was open for 2% of the time, Pallas kernels for 0%

profile of v1, /device:TPU:13, one launch (start us, length us, event | category | flops | bytes accessed | tf_op | source)
XLA Modules:
  0.0 490.1 jit_solution(3457433711483088804)
XLA Ops:
  6.5 0.7 convert_element_type.41
  7.2 4.8 fusion.21
  12.1 109.1 %all-reduce.4.cloned.1.call-done = f32[1024,1024]{1,0:T(8,128)} async-done(((f32[1024,1024]{1,0:T(8,128)}), f32[1024,1024]{1,0:T(8,128)}) %all-reduce.4.cloned.1.call-update) | async-done | bytes 4194320 | tf_op jit(solution)/shard_map/psum | solution.py:63
  121.2 114.4 %all-reduce.6.cloned.1.call-done = f32[1024,1024]{1,0:T(8,128)} async-done(((f32[1024,1024]{1,0:T(8,128)}), f32[1024,1024]{1,0:T(8,128)}) %all-reduce.6.cloned.1.call-update) | async-done | bytes 4194320 | tf_op jit(solution)/shard_map/psum | solution.py:63
  235.6 2.6 abs_reduce_fusion
  238.8 5.7 %subtract_multiply_fusion = (f32[1024,1024]{1,0:T(8,128)}, f32[1024,1024]{1,0:T(8,128)S(1)}) fusion(f32[1024,1024]{1,0:T(8,128)} %all-reduce.6.cloned.1.call-done, f32[]{:T(128)} %reduce_max.9), kind=kLoop, calls=%fused_computation.6 | loop fusion | flops 5242880 | bytes 12582916 | tf_op jit(solution)/shard_map/mul | solution.py:65
  244.5 8.4 %subtract_multiply_fusion.1 = f32[512,1024]{1,0:T(8,128)} fusion(f32[1024,1024]{1,0:T(8,128)S(1)} %get-tuple-element.6, s32[]{:T(128)S(6)} %select_n.20), kind=kOutput, calls=%fused_computation.18 | convolution fusion | flops 6444023808 | bytes 10486784 | tf_op jit(solution)/shard_map/dot_general | solution.py:44
  253.2 56.7 %all-gather.3.cloned.1.call-done = f32[1024,1024]{1,0:T(8,128)} async-done(((f32[512,1024]{1,0:T(8,128)}), f32[1024,1024]{1,0:T(8,128)}) %all-gather.3.cloned.1.call-update) | async-done | bytes 4194320 | tf_op jit(solution)/shard_map/all_gather | solution.py:68
  309.9 10.0 %fusion.10 = f32[512,1024]{1,0:T(8,128)S(1)} fusion(f32[1024,1024]{1,0:T(8,128)} %all-gather.3.cloned.1.call-done, f32[1024,1024]{1,0:T(8,128)} %get-tuple-element.5, s32[]{:T(128)S(6)} %select_n.20), kind=kOutput, calls=%fused_computation.22 | convolution fusion | flops 6442450944 | bytes 8388612 | tf_op jit(solution)/shard_map/dot_general | solution.py:49
  319.9 8.0 %multiply_convert_fusion.1 = bf16[512,1024]{1,0:T(8,128)(2,1)} fusion(f32[1024,1024]{1,0:T(8,128)S(1)} %copy-done, s32[]{:T(128)S(6)} %select_n.20, f32[512,1024]{1,0:T(8,128)S(1)} %fusion.10), kind=kOutput, calls=%fused_computation.17 | convolution fusion | flops 6444548096 | bytes 9437188 | tf_op jit(solution)/shard_map/dot_general | solution.py:50
  328.1 0.9 reduce-window.6
  329.3 2.8 scatter_custom_fusion.1
  332.8 6.4 %all-to-all-start.1 = ((bf16[16,1,64]{2,1,0:T(2,128)(2,1)}), bf16[16,1,64]{2,1,0:T(2,128)(2,1)S(1)}, u32[]{:S(2)}, u32[]{:S(2)}) async-start(bf16[16,1,64]{2,1,0:T(2,128)(2,1)} %all_to_all.16), calls=%async_computation.1 | async-start | bytes 16384 | tf_op jit(solution)/shard_map/all_to_all | solution.py:84
  339.1 22.1 %all-gather.5.cloned.1.call-done = bf16[1024,1024]{1,0:T(8,128)(2,1)} async-done(((bf16[512,1024]{1,0:T(8,128)(2,1)}), bf16[1024,1024]{1,0:T(8,128)(2,1)}) %all-gather.5.cloned.1.call-update) | async-done | bytes 2097168 | tf_op jit(solution)/shard_map/all_gather | solution.py:69
  361.3 2.6 multiply_reduce_fusion.1
  363.9 3.7 scatter_custom_fusion
  367.6 6.4 %all-to-all-start = ((bf16[16,64,1024]{2,1,0:T(8,128)(2,1)}), bf16[16,64,1024]{2,1,0:T(8,128)(2,1)S(1)}, u32[]{:S(2)}, u32[]{:S(2)}) async-start(bf16[16,64,1024]{2,1,0:T(8,128)(2,1)} %bitcast.2), calls=%async_computation | async-start | bytes 4194304 | tf_op jit(solution)/shard_map/all_to_all | solution.py:77
  374.0 47.3 %all-to-all-done = bf16[16,64,1024]{2,1,0:T(8,128)(2,1)S(1)} async-done(((bf16[16,64,1024]{2,1,0:T(8,128)(2,1)}), bf16[16,64,1024]{2,1,0:T(8,128)(2,1)S(1)}, u32[]{:S(2)}, u32[]{:S(2)}) %all-to-all-start) | async-done | bytes 2097184 | tf_op jit(solution)/shard_map/all_to_all | solution.py:77
  421.4 2.7 fusion
  424.1 2.7 multiply_reduce_fusion
  426.8 1.8 multiply_convert_fusion
  428.6 4.9 %all-to-all-start.2 = ((bf16[16,64,1024]{2,1,0:T(8,128)(2,1)}), bf16[16,64,1024]{2,1,0:T(8,128)(2,1)S(1)}, u32[]{:S(2)}, u32[]{:S(2)}) async-start(bf16[16,64,1024]{2,1,0:T(8,128)(2,1)} %bitcast.30), calls=%async_computation.2 | async-start | bytes 4194304 | tf_op jit(solution)/shard_map/all_to_all | solution.py:95
  433.5 47.4 %all-to-all-done.2 = bf16[16,64,1024]{2,1,0:T(8,128)(2,1)S(1)} async-done(((bf16[16,64,1024]{2,1,0:T(8,128)(2,1)}), bf16[16,64,1024]{2,1,0:T(8,128)(2,1)S(1)}, u32[]{:S(2)}, u32[]{:S(2)}) %all-to-all-start.2) | async-done | bytes 2097184 | tf_op jit(solution)/shard_map/all_to_all | solution.py:95
  481.0 2.7 gather_fusion
  (31 shorter events, 2.2 us)
Async XLA Ops:
  6.5 114.6 %all-reduce.4.cloned.1.call-start = ((), (), s32[]{:S(2)}) async-start(), calls=%async_computation.3 | async-start | bytes 8388608 | tf_op jit(solution)/shard_map/psum | solution.py:63
  12.0 223.6 %all-reduce.6.cloned.1.call-start = ((), (), s32[]{:S(2)}) async-start(), calls=%async_computation.4 | async-start | bytes 8388608 | tf_op jit(solution)/shard_map/psum | solution.py:63
  121.2 188.7 %all-gather.3.cloned.1.call-start = ((), (), s32[]{:S(2)}) async-start(), calls=%async_computation.5 | async-start | bytes 6291456 | tf_op jit(solution)/shard_map/all_gather | solution.py:68
  252.9 108.3 %all-gather.5.cloned.1.call-start = ((), (), s32[]{:S(2)}) async-start(), calls=%async_computation.6 | async-start | bytes 3145728 | tf_op jit(solution)/shard_map/all_gather | solution.py:69
  309.9 10.0 %copy-start = (f32[1024,1024]{1,0:T(8,128)S(1)}, f32[1024,1024]{1,0:T(8,128)}, u32[]{:S(2)}) copy-start(f32[1024,1024]{1,0:T(8,128)} %get-tuple-element.5) | copy-start | bytes 12582916
  319.9 8.1 %copy-start.2 = (s32[352,1]{0,1:T(1,128)S(1)}, s32[352,1]{0,1:T(1,128)}, u32[]{:S(2)}) copy-start(s32[352,1]{0,1:T(1,128)} %param.4) | copy-start | bytes 4228
  319.9 41.4 %copy-start.1 = (bf16[352,1024]{1,0:T(8,128)(2,1)S(1)}, bf16[352,1024]{1,0:T(8,128)(2,1)}, u32[]{:S(2)}) copy-start(bf16[352,1024]{1,0:T(8,128)(2,1)} %param.3) | copy-start | bytes 2162692
  332.8 34.8 %all-to-all-start.1 = ((bf16[16,1,64]{2,1,0:T(2,128)(2,1)}), bf16[16,1,64]{2,1,0:T(2,128)(2,1)S(1)}, u32[]{:S(2)}, u32[]{:S(2)}) async-start(bf16[16,1,64]{2,1,0:T(2,128)(2,1)} %all_to_all.16), calls=%async_computation.1 | async-start | bytes 16384 | tf_op jit(solution)/shard_map/all_to_all | solution.py:84
  367.6 53.8 %all-to-all-start = ((bf16[16,64,1024]{2,1,0:T(8,128)(2,1)}), bf16[16,64,1024]{2,1,0:T(8,128)(2,1)S(1)}, u32[]{:S(2)}, u32[]{:S(2)}) async-start(bf16[16,64,1024]{2,1,0:T(8,128)(2,1)} %bitcast.2), calls=%async_computation | async-start | bytes 4194304 | tf_op jit(solution)/shard_map/all_to_all | solution.py:77
  428.6 52.3 %all-to-all-start.2 = ((bf16[16,64,1024]{2,1,0:T(8,128)(2,1)}), bf16[16,64,1024]{2,1,0:T(8,128)(2,1)S(1)}, u32[]{:S(2)}, u32[]{:S(2)}) async-start(bf16[16,64,1024]{2,1,0:T(8,128)(2,1)} %bitcast.30), calls=%async_computation.2 | async-start | bytes 4194304 | tf_op jit(solution)/shard_map/all_to_all | solution.py:95
Sparse Core Ops, SparseCore 0:
  12.1 108.9 all-reduce.3
  125.3 110.2 all-reduce.5
  253.1 56.7 all-gather.2
  328.1 33.1 all-gather.4
